TPU v7x, 32 devices: a whole 2x2x4 slice. The times are simulated.
32 devices in a mesh: grp: 2 (over y), row: 4 (over z), col: 4 (over x, core).
Axes of the slice: x: 2, y: 2, z: 4, core: 2. Of those that a mesh axis runs over, the one named last changes fastest.
Arguments:
- group_rhs: float32 [2, 1024, 128], P('grp', 'row'), may hold values from -6 to 6
- group_lower: float32 [2, 1024, 1024], P('grp', 'row', 'col'), may hold values from -0.09375 to 0.09375
- group_diag_inv: float32 [2, 1024, 256], P('grp'), as said below
- group_offdiag: float32 [2, 1024, 1024], P('grp', 'row', 'col'), may hold values from -0.09375 to 0.09375
- group_rows: int32 [2, 1024], P('grp', 'row'), may hold values from 0 to 2047, as said below
- root_rhs: float32 [2048, 128], P(('grp', 'row', 'col')), may hold values from -6 to 6
- root_lower: float32 [2048, 2048], P(('grp', 'row'), 'col'), may hold values from -0.0625 to 0.0625
- root_diag_inv: float32 [2048, 512], replicated, as said below
Outputs:
- group_solution: float32 [2, 1024, 128], P('grp', 'row')
- root_solution: float32 [2048, 128], P(('grp', 'row', 'col'))
Inputs may be any that keep to these rules, and one draw needn't show every extreme that they name: `group_rows`: within one group the rows are distinct and ascending. `group_diag_inv`: each stacked block is lower triangular with diagonal entries between 0.5 and 1.5. `root_diag_inv`: each stacked block is lower triangular with diagonal entries between 0.5 and 1.5.
All inputs are finite; a program needn't handle non-finite values.
Results may differ from a plain program's by a relative error of at most 0.0001.
Values sent between devices are 32-bit elements; how exact they have to be, the bound alone decides.
A program may use at most 64 MiB of HBM per device.

v0:
```python
import jax
import jax.numpy as jnp
from jax import lax
from jax.sharding import PartitionSpec as P


def exact_dot(left, right):
    return jnp.dot(left, right, precision=lax.Precision.HIGHEST, preferred_element_type=jnp.float32)


def exact_tdot(left, right):
    return lax.dot_general(
        left,
        right,
        (((0,), (0,)), ((), ())),
        precision=lax.Precision.HIGHEST,
        preferred_element_type=jnp.float32,
    )


def forward_total(contrib):
    return lax.psum(contrib, ("row", "col"))


def backward_total(contrib):
    return lax.psum(contrib, ("row", "col"))


def local(
    group_rhs,
    group_lower,
    group_diag_inv,
    group_offdiag,
    group_rows,
    root_rhs,
    root_lower,
    root_diag_inv,
):
    row_count = lax.axis_size("row")
    col_count = lax.axis_size("col")
    my_row = lax.axis_index("row")
    my_col = lax.axis_index("col")
    my_grp = lax.axis_index("grp")
    own_rhs = group_rhs[0]
    own_lower = group_lower[0]
    own_inv = group_diag_inv[0]
    own_offdiag = group_offdiag[0]
    own_rows = group_rows[0]
    span_rows = own_lower.shape[0]
    columns = own_rhs.shape[1]
    root_width = root_diag_inv.shape[0]
    root_span = root_diag_inv.shape[1]
    strip_rows = root_lower.shape[0]
    piece_rows = root_rhs.shape[0]
    zero_block = jnp.zeros((span_rows, columns), jnp.float32)
    zero_root = jnp.zeros((root_span, columns), jnp.float32)
    group_y = jnp.zeros((row_count * span_rows, columns), jnp.float32)
    for kblock in range(row_count):
        known = lax.dynamic_slice_in_dim(group_y, my_col * span_rows, span_rows, 0)
        contrib = jnp.where(my_col < kblock, -exact_dot(own_lower, known), zero_block)
        contrib = contrib + jnp.where(my_col == 0, own_rhs, zero_block)
        contrib = jnp.where(my_row == kblock, contrib, zero_block)
        summed = forward_total(contrib)
        solved_block = exact_dot(own_inv[kblock * span_rows : (kblock + 1) * span_rows], summed)
        group_y = group_y.at[kblock * span_rows : (kblock + 1) * span_rows].set(solved_block)
    own_y = lax.dynamic_slice_in_dim(group_y, my_col * span_rows, span_rows, 0)
    partial_update = exact_dot(own_offdiag, own_y)
    spread_update = jnp.zeros((root_width, columns), jnp.float32).at[own_rows].add(partial_update)
    flat_index = (my_grp * row_count + my_row) * col_count + my_col
    placed = lax.dynamic_update_slice_in_dim(
        jnp.zeros_like(spread_update), root_rhs, flat_index * piece_rows, 0
    )
    root_side = lax.psum(placed - spread_update, ("grp", "row", "col"))
    root_y = jnp.zeros((root_width, columns), jnp.float32)
    root_x = jnp.zeros((root_width, columns), jnp.float32)
    strip_start = (my_grp * row_count + my_row) * strip_rows
    strip_block = strip_start // root_span
    strip_offset = strip_start - strip_block * root_span
    for kblock in range(col_count):
        known = lax.dynamic_slice_in_dim(root_y, my_col * root_span, root_span, 0)
        partial_rows = jnp.where(
            (strip_block == kblock) & (my_col < kblock), exact_dot(root_lower, known), 0.0
        )
        contrib = lax.dynamic_update_slice_in_dim(zero_root, partial_rows, strip_offset, 0)
        summed = lax.psum(contrib, ("grp", "row", "col"))
        first_row = kblock * root_span
        solved_block = exact_dot(
            root_diag_inv[first_row : first_row + root_span],
            root_side[first_row : first_row + root_span] - summed,
        )
        root_y = root_y.at[first_row : first_row + root_span].set(solved_block)
    for kblock in reversed(range(col_count)):
        known = lax.dynamic_slice_in_dim(root_x, strip_start, strip_rows, 0)
        contrib = jnp.where(
            (strip_block > kblock) & (my_col == kblock), exact_tdot(root_lower, known), zero_root
        )
        summed = lax.psum(contrib, ("grp", "row", "col"))
        first_row = kblock * root_span
        solved_block = exact_tdot(
            root_diag_inv[first_row : first_row + root_span],
            root_y[first_row : first_row + root_span] - summed,
        )
        root_x = root_x.at[first_row : first_row + root_span].set(solved_block)
    picked = jnp.take(root_x, own_rows, axis=0)
    lifted = exact_tdot(own_offdiag, picked)
    group_x = jnp.zeros((row_count * span_rows, columns), jnp.float32)
    for kblock in reversed(range(row_count)):
        known = lax.dynamic_slice_in_dim(group_x, my_row * span_rows, span_rows, 0)
        contrib = jnp.where(my_row > kblock, -exact_tdot(own_lower, known), zero_block) - lifted
        contrib = contrib + jnp.where(
            my_row == 0, group_y[kblock * span_rows : (kblock + 1) * span_rows], zero_block
        )
        contrib = jnp.where(my_col == kblock, contrib, zero_block)
        summed = backward_total(contrib)
        solved_block = exact_tdot(own_inv[kblock * span_rows : (kblock + 1) * span_rows], summed)
        group_x = group_x.at[kblock * span_rows : (kblock + 1) * span_rows].set(solved_block)
    group_out = lax.dynamic_slice_in_dim(group_x, my_row * span_rows, span_rows, 0)[None]
    root_out = lax.dynamic_slice_in_dim(root_x, flat_index * piece_rows, piece_rows, 0)
    return (group_out, root_out)


def solution(mesh):
    placed = (
        P("grp", "row", None),
        P("grp", "row", "col"),
        P("grp", None, None),
        P("grp", "row", "col"),
        P("grp", "row"),
        P(("grp", "row", "col"), None),
        P(("grp", "row"), "col"),
        P(),
    )
    return jax.shard_map(
        local,
        mesh=mesh,
        in_specs=placed,
        out_specs=(P("grp", "row", None), P(("grp", "row", "col"), None)),
        check_vma=False,
    )
```

profile of v0, /device:TPU:0, one launch (start us, length us, event | category | flops | bytes accessed | tf_op | source)
XLA Modules:
  0.0 1688.2 jit_solution(14980410069233360263)
XLA Ops:
  8.4 2.1 fusion.48
  11.2 90.5 %all-reduce.22.cloned.1.call-done = f32[256,128]{0,1:T(8,128)} async-done(((f32[256,128]{0,1:T(8,128)}), f32[256,128]{0,1:T(8,128)}) %all-reduce.22.cloned.1.call-update) | async-done | bytes 131088 | tf_op jit(solution)/shard_map/psum | solution.py:22
  103.2 2.0 fusion.44
  106.1 88.3 %all-reduce.24.cloned.1.call-done = f32[256,128]{0,1:T(8,128)} async-done(((f32[256,128]{0,1:T(8,128)}), f32[256,128]{0,1:T(8,128)}) %all-reduce.24.cloned.1.call-update) | async-done | bytes 131088 | tf_op jit(solution)/shard_map/psum | solution.py:22
  197.1 90.1 %all-reduce.26.cloned.1.call-done = f32[256,128]{0,1:T(8,128)} async-done(((f32[256,128]{0,1:T(8,128)}), f32[256,128]{0,1:T(8,128)}) %all-reduce.26.cloned.1.call-update) | async-done | bytes 131088 | tf_op jit(solution)/shard_map/psum | solution.py:22
  291.3 88.4 %all-reduce.28.cloned.1.call-done = f32[256,128]{0,1:T(8,128)} async-done(((f32[256,128]{0,1:T(8,128)}), f32[256,128]{0,1:T(8,128)}) %all-reduce.28.cloned.1.call-update) | async-done | bytes 131088 | tf_op jit(solution)/shard_map/psum | solution.py:22
  379.7 2.0 constant_dynamic-update-slice_fusion.5
  383.8 2.3 sub.58
  386.3 133.3 %all-reduce.50.cloned.1.call-done = (f32[512,128]{1,0:T(8,128)}, f32[2048,128]{1,0:T(8,128)}) async-done(((f32[512,128]{1,0:T(8,128)}, f32[2048,128]{1,0:T(8,128)}), (f32[512,128]{1,0:T(8,128)}, f32[2048,128]{1,0:T(8,128)})) %all-reduce.50.cloned.1.call-update) | async-done | bytes 1310736 | tf_op jit(solution)/shard_map/psum | solution.py:85
  519.6 2.6 convolution_bitcast_fusion.7
  525.6 123.3 %all-reduce.30.cloned.1.call-done = f32[512,128]{1,0:T(8,128)} async-done(((f32[512,128]{1,0:T(8,128)}), f32[512,128]{1,0:T(8,128)}) %all-reduce.30.cloned.1.call-update) | async-done | bytes 262160 | tf_op jit(solution)/shard_map/psum | solution.py:85
  648.9 2.6 fusion.7
  656.5 123.0 %all-reduce.32.cloned.1.call-done = f32[512,128]{1,0:T(8,128)} async-done(((f32[512,128]{1,0:T(8,128)}), f32[512,128]{1,0:T(8,128)}) %all-reduce.32.cloned.1.call-update) | async-done | bytes 262160 | tf_op jit(solution)/shard_map/psum | solution.py:85
  779.4 3.3 constant_dynamic-update-slice_fusion.1
  786.7 127.0 %all-reduce.48.cloned.1.call-done = (f32[512,128]{0,1:T(8,128)}, f32[512,128]{1,0:T(8,128)}) async-done(((f32[512,128]{0,1:T(8,128)}, f32[512,128]{1,0:T(8,128)}), (f32[512,128]{0,1:T(8,128)}, f32[512,128]{1,0:T(8,128)})) %all-reduce.48.cloned.1.call-update) | async-done | bytes 524304 | tf_op jit(solution)/shard_map/psum | solution.py:97
  913.8 2.7 fusion.8
  916.5 1.9 convolution_bitcast_fusion.3
  921.4 123.0 %all-reduce.34.cloned.1.call-done = f32[512,128]{0,1:T(8,128)} async-done(((f32[512,128]{0,1:T(8,128)}), f32[512,128]{0,1:T(8,128)}) %all-reduce.34.cloned.1.call-update) | async-done | bytes 262160 | tf_op jit(solution)/shard_map/psum | solution.py:97
  1044.5 2.1 fusion.6
  1047.8 127.0 %all-reduce.36.cloned.1.call-done = f32[512,128]{0,1:T(8,128)} async-done(((f32[512,128]{0,1:T(8,128)}), f32[512,128]{0,1:T(8,128)}) %all-reduce.36.cloned.1.call-update) | async-done | bytes 262160 | tf_op jit(solution)/shard_map/psum | solution.py:97
  1174.8 2.1 fusion.5
  1178.1 127.1 %all-reduce.38.cloned.1.call-done = f32[512,128]{0,1:T(8,128)} async-done(((f32[512,128]{0,1:T(8,128)}), f32[512,128]{0,1:T(8,128)}) %all-reduce.38.cloned.1.call-update) | async-done | bytes 262160 | tf_op jit(solution)/shard_map/psum | solution.py:97
  1305.2 2.1 fusion.4
  1308.7 2.6 gather_fusion
  1312.7 1.9 fusion.53
  1314.7 85.2 %all-reduce.40.cloned.1.call-done = f32[256,128]{0,1:T(8,128)} async-done(((f32[256,128]{0,1:T(8,128)}), f32[256,128]{0,1:T(8,128)}) %all-reduce.40.cloned.1.call-update) | async-done | bytes 131088 | tf_op jit(solution)/shard_map/psum | solution.py:26
  1404.5 87.8 %all-reduce.42.cloned.1.call-done = f32[256,128]{0,1:T(8,128)} async-done(((f32[256,128]{0,1:T(8,128)}), f32[256,128]{0,1:T(8,128)}) %all-reduce.42.cloned.1.call-update) | async-done | bytes 131088 | tf_op jit(solution)/shard_map/psum | solution.py:26
  1492.3 1.9 fusion.21
  1496.1 89.1 %all-reduce.44.cloned.1.call-done = f32[256,128]{0,1:T(8,128)} async-done(((f32[256,128]{0,1:T(8,128)}), f32[256,128]{0,1:T(8,128)}) %all-reduce.44.cloned.1.call-update) | async-done | bytes 131088 | tf_op jit(solution)/shard_map/psum | solution.py:26
  1585.2 1.9 fusion.15
  1589.7 88.4 %all-reduce.46.cloned.1.call-done = f32[256,128]{0,1:T(8,128)} async-done(((f32[256,128]{0,1:T(8,128)}), f32[256,128]{0,1:T(8,128)}) %all-reduce.46.cloned.1.call-update) | async-done | bytes 131088 | tf_op jit(solution)/shard_map/psum | solution.py:26
  1678.1 1.9 fusion.9
  (102 shorter events, 44.2 us)
Async XLA Ops:
  7.2 3.4 copy-start
  7.2 188.7 %copy-start.1 = (f32[1,256,256]{2,1,0:T(8,128)S(1)}, f32[1,256,256]{2,1,0:T(8,128)}, u32[]{:S(2)}) copy-start(f32[1,256,256]{2,1,0:T(8,128)} %param.41) | copy-start | bytes 786436
  7.2 280.0 %copy-start.2 = (f32[1,1024,256]{2,1,0:T(8,128)S(1)}, f32[1,1024,256]{2,1,0:T(8,128)}, u32[]{:S(2)}) copy-start(f32[1,1024,256]{2,1,0:T(8,128)} %param.42) | copy-start | bytes 3145732
  7.2 283.4 %copy-start.10 = (f32[64,128]{1,0:T(8,128)S(1)}, f32[64,128]{1,0:T(8,128)}, u32[]{:S(2)}) copy-start(f32[64,128]{1,0:T(8,128)} %param.45) | copy-start | bytes 98308
  7.2 94.6 %all-reduce.22.cloned.1.call-start = ((), (), s32[]{:S(2)}) async-start(), calls=%async_computation | async-start | bytes 262144 | tf_op jit(solution)/shard_map/psum | solution.py:22
  8.4 373.3 %copy-start.7 = (f32[1,256,256]{2,1,0:T(8,128)S(1)}, f32[1,256,256]{2,1,0:T(8,128)}, u32[]{:S(2)}) copy-start(f32[1,256,256]{2,1,0:T(8,128)} %param.43) | copy-start | bytes 786436
  10.5 184.0 %all-reduce.24.cloned.1.call-start = ((), (), s32[]{:S(2)}) async-start(), calls=%async_computation.1 | async-start | bytes 262144 | tf_op jit(solution)/shard_map/psum | solution.py:22
  105.2 181.9 %all-reduce.26.cloned.1.call-start = ((), (), s32[]{:S(2)}) async-start(), calls=%async_computation.2 | async-start | bytes 262144 | tf_op jit(solution)/shard_map/psum | solution.py:22
  197.0 182.7 %all-reduce.28.cloned.1.call-start = ((), (), s32[]{:S(2)}) async-start(), calls=%async_computation.3 | async-start | bytes 262144 | tf_op jit(solution)/shard_map/psum | solution.py:22
  197.1 185.1 %copy-start.8 = (f32[512,128]{1,0:T(8,128)}, f32[512,128]{1,0:T(8,128)S(1)}, u32[]{:S(2)}) copy-start(f32[512,128]{1,0:T(8,128)S(1)} %constant_dynamic-update-slice_fusion.4) | copy-start | bytes 786436
  289.5 230.0 %all-reduce.50.cloned.1.call-start = ((), (), s32[]{:S(2)}) async-start(), calls=%async_computation.14 | async-start | bytes 2621440 | tf_op jit(solution)/shard_map/psum | solution.py:85
  386.2 262.7 %all-reduce.30.cloned.1.call-start = ((), (), s32[]{:S(2)}) async-start(), calls=%async_computation.4 | async-start | bytes 524288 | tf_op jit(solution)/shard_map/psum | solution.py:85
  522.2 0.7 copy-start.4
  523.7 0.7 copy-start.9
  524.5 254.9 %all-reduce.32.cloned.1.call-start = ((), (), s32[]{:S(2)}) async-start(), calls=%async_computation.5 | async-start | bytes 524288 | tf_op jit(solution)/shard_map/psum | solution.py:85
  655.3 258.5 %all-reduce.48.cloned.1.call-start = ((), (), s32[]{:S(2)}) async-start(), calls=%async_computation.13 | async-start | bytes 1048576 | tf_op jit(solution)/shard_map/psum | solution.py:97
  782.8 137.6 %copy-start.3 = (f32[2048,128]{0,1:T(8,128)}, f32[2048,128]{0,1:T(8,128)S(1)}, u32[]{:S(2)}) copy-start(f32[2048,128]{0,1:T(8,128)S(1)} %get-tuple-element.204) | copy-start | bytes 3145732
  786.5 258.0 %all-reduce.34.cloned.1.call-start = ((), (), s32[]{:S(2)}) async-start(), calls=%async_computation.6 | async-start | bytes 524288 | tf_op jit(solution)/shard_map/psum | solution.py:97
  918.4 0.7 copy-start.5
  919.1 259.0 %copy-start.11 = (s32[1,256]{1,0:T(1,128)S(1)}, s32[1,256]{1,0:T(1,128)}, u32[]{:S(2)}) copy-start(s32[1,256]{1,0:T(1,128)} %param.44) | copy-start | bytes 3076
  920.3 254.5 %all-reduce.36.cloned.1.call-start = ((), (), s32[]{:S(2)}) async-start(), calls=%async_computation.7 | async-start | bytes 524288 | tf_op jit(solution)/shard_map/psum | solution.py:97
  1047.7 257.5 %all-reduce.38.cloned.1.call-start = ((), (), s32[]{:S(2)}) async-start(), calls=%async_computation.8 | async-start | bytes 524288 | tf_op jit(solution)/shard_map/psum | solution.py:97
  1178.0 221.8 %all-reduce.40.cloned.1.call-start = ((), (), s32[]{:S(2)}) async-start(), calls=%async_computation.9 | async-start | bytes 262144 | tf_op jit(solution)/shard_map/psum | solution.py:26
  1314.6 177.7 %all-reduce.42.cloned.1.call-start = ((), (), s32[]{:S(2)}) async-start(), calls=%async_computation.10 | async-start | bytes 262144 | tf_op jit(solution)/shard_map/psum | solution.py:26
  1401.0 0.7 copy-start.6
  1402.6 182.6 %all-reduce.44.cloned.1.call-start = ((), (), s32[]{:S(2)}) async-start(), calls=%async_computation.11 | async-start | bytes 262144 | tf_op jit(solution)/shard_map/psum | solution.py:26
  1496.0 182.1 %all-reduce.46.cloned.1.call-start = ((), (), s32[]{:S(2)}) async-start(), calls=%async_computation.12 | async-start | bytes 262144 | tf_op jit(solution)/shard_map/psum | solution.py:26
Sparse Core Ops, SparseCore 0:
  12.1 89.6 all-reduce.21
  105.8 88.6 all-reduce.23
  198.5 88.6 all-reduce.25
  291.0 88.6 all-reduce.27
  386.3 133.2 all-reduce.49
  524.9 123.9 all-reduce.29
  655.4 123.9 all-reduce.31
  786.6 127.1 all-reduce.47
  920.4 124.0 all-reduce.33
  1050.7 124.0 all-reduce.35
  1181.2 123.9 all-reduce.37
  1314.7 85.0 all-reduce.39
  1403.7 88.5 all-reduce.41
  1496.6 88.5 all-reduce.43
  1589.5 88.5 all-reduce.45
where the time goes:
time: 1690 us
  waiting for transfers between devices  1590 us (94%)
  matrix products  55.5 us (3%)
  local copies, waits for them, and re-layouts  20.9 us (1%)
    psum x7, waiting for transfers between devices, local(): summed = lax.psum(contrib, ('grp', 'row', 'col'))  884 us
    psum x4, waiting for transfers between devices, forward_total(): return lax.psum(contrib, ('row', 'col'))  357 us
    psum x4, waiting for transfers between devices, backward_total(): return lax.psum(contrib, ('row', 'col'))  350 us
  transfers between devices with their start and end apart: 15, of which 15 were waited for; matrix products, arithmetic and copies ran while one was open for 1% of the time, Pallas kernels for 0%

commit v1 on v0

v1 whole, which is shorter than its diff:
```python
import functools

import jax
import jax.numpy as jnp
from jax import lax
from jax.experimental import pallas as pl
from jax.experimental.pallas import tpu as pltpu
from jax.sharding import PartitionSpec as P

CORES = 2
MESH = pl.DeviceIdType.MESH
VMEM_BYTES = 56 * 1024 * 1024


def split(a):
    high = a.astype(jnp.bfloat16)
    low = (a - high.astype(jnp.float32)).astype(jnp.bfloat16)
    return high, low


def bdot(a, b):
    return jnp.dot(a, b, preferred_element_type=jnp.float32)


def mm(a, b):
    ah, al = split(a)
    n = b.shape[1]
    w = jnp.concatenate(split(b), axis=1)
    both = bdot(ah, w) + bdot(al, w)
    return both[:, :n] + both[:, n:]


def tmm(xt, a):
    ah, al = split(a)
    n = xt.shape[0]
    v = jnp.concatenate(split(xt), axis=0)
    both = bdot(v, ah) + bdot(v, al)
    return both[:n] + both[n:]


class Sizes:
    def __init__(self, mesh_shape):
        self.G, self.R, self.C = mesh_shape["grp"], mesh_shape["row"], mesh_shape["col"]
        self.X = self.C // CORES


def here():
    return lax.axis_index("grp"), lax.axis_index("row"), lax.axis_index("col")


def remote(src, dst, ss, rs, dev):
    cp = pltpu.make_async_remote_copy(
        src_ref=src, dst_ref=dst, send_sem=ss, recv_sem=rs, device_id=dev, device_id_type=MESH
    )
    cp.start()
    return cp


def wait_on(ref, sem):
    pltpu.make_async_copy(ref, ref, sem).wait()


def greet(devs):
    barrier = pltpu.get_barrier_semaphore()
    for dev in devs:
        pl.semaphore_signal(barrier, inc=1, device_id=dev, device_id_type=MESH)
    pl.semaphore_wait(barrier, len(devs))


class Sems:
    def __init__(self, send, recv):
        self.send, self.recv, self.at = send, recv, 0

    def next(self):
        k = self.at
        self.at += 1
        return self.send.at[k], self.recv.at[k]


def plane_offsets(z):
    return [(dg, dx) for dg in range(z.G) for dx in range(z.X) if dg or dx]


def row_send(z, src, slot, sems):
    g, r, c = here()
    waits = []
    for d in range(1, z.R):
        ss, rs = sems.next()
        cp = remote(src, slot(r), ss, rs, (g, (r + d) % z.R, c))
        waits.append((cp, slot((r - d + z.R) % z.R), rs))
    return waits


def plane_send(z, slot, sems, offsets=None):
    g, r, c = here()
    x, core = c // CORES, c % CORES
    waits = []
    for dg, dx in plane_offsets(z) if offsets is None else offsets:
        ss, rs = sems.next()
        tg, tx = (g + dg) % z.G, (x + dx) % z.X
        fg, fx = (g - dg + z.G) % z.G, (x - dx + z.X) % z.X
        cp = remote(slot(g, x), slot(g, x), ss, rs, (tg, r, tx * CORES + core))
        waits.append((cp, slot(fg, fx), rs))
    return waits


def core_send(z, slot, sems):
    g, r, c = here()
    x, core = c // CORES, c % CORES
    ss, rs = sems.next()
    cp = remote(slot(core), slot(core), ss, rs, (g, r, x * CORES + 1 - core))
    return [(cp, slot(1 - core), rs)]


def arrive(waits):
    for _, ref, rs in waits:
        wait_on(ref, rs)


def sent(waits):
    for cp, _, _ in waits:
        cp.wait_send()


def pair_count(n):
    return n * (n - 1) // 2


def gather_kernel(z, spb, with_root, refs_in, refs_out, send, recv, keep):
    g, r, c = here()
    x, core = c // CORES, c % CORES
    glow, grhs, rows, rrhs = refs_in[:4]
    GL, GR, ROWS, RR = refs_out[:4]
    sems = Sems(send, recv)
    if with_root:
        devs = [
            ((g + dg) % z.G, (r + dr) % z.R, (c + dc) % z.C)
            for dg in range(z.G) for dr in range(z.R) for dc in range(z.C) if dg or dr or dc
        ]
    else:
        devs = [
            (g, (r + dr) % z.R, (c + dc) % z.C)
            for dr in range(z.R) for dc in range(z.C) if dr or dc
        ]
        devs += [
            ((g + dg) % z.G, r, (x + dx) % z.X * CORES + core)
            for dg, dx in plane_offsets(z) if dg
        ]
    greet(devs)

    locals_ = []
    for k, (src, dst) in enumerate(
        ((grhs, GR.at[r]), (rows, ROWS.at[g, r]), (rrhs, RR.at[core, g, x, r]))
    ):
        cp = pltpu.make_async_copy(src, dst, keep.at[k])
        cp.start()
        locals_.append(cp)

    def scatter(src, out_slot, holder, idx, n_pieces, groups):
        base = sems.at
        rows_each = out_slot(0, 0, 0, 0).shape[0]
        offs = [
            (dg, dr, dc)
            for dg in (range(z.G) if groups else (0,)) for dr in range(z.R) for dc in range(z.C)
        ]
        sems.at += max(n_pieces, len(offs))

        def chunk(tg, tc):
            tx, tcore = tc // CORES, tc % CORES
            q = (tcore * z.G + tg) * z.X + tx if groups else tcore * z.X + tx
            return src.at[pl.ds(pl.multiple_of(q * rows_each, 8), rows_each)]

        def copies(start):
            for k, (dg, dr, dc) in enumerate(offs):
                tg, tr, tc = (g + dg) % z.G, (r + dr) % z.R, (c + dc) % z.C
                dst = out_slot(tc % CORES, tg, tc // CORES, idx)
                if dg or dr or dc:
                    cp = pltpu.make_async_remote_copy(
                        src_ref=chunk(tg, tc), dst_ref=dst, send_sem=send.at[base + k],
                        recv_sem=recv.at[base + idx], device_id=(tg, tr, tc), device_id_type=MESH,
                    )
                    cp.start() if start else cp.wait_send()
                elif start:
                    pltpu.make_async_copy(chunk(tg, tc), dst, recv.at[base + idx]).start()

        @pl.when(holder)
        def _():
            copies(True)

        def received():
            for k in range(n_pieces):
                wait_on(out_slot(core, g, x, k), recv.at[base + k])

        def done():
            @pl.when(holder)
            def _():
                copies(False)

        return received, done

    rhs_w = row_send(z, grhs, lambda rr: GR.at[rr], sems)
    rows_w = row_send(z, rows, lambda rr: ROWS.at[g, rr], sems)
    rr_w = row_send(z, rrhs, lambda rr: RR.at[core, g, x, rr], sems)
    gl_recv, gl_done = scatter(
        glow, lambda a, b, d, k: GL.at[a, d, k], c < r, r * (r - 1) // 2 + c, pair_count(z.R), False
    )
    if with_root:
        rlow, RL = refs_in[4], refs_out[4]
        strip = g * z.R + r
        kb = strip // spb
        idx = spb * (kb * (kb - 1) // 2) + (strip - kb * spb) * kb + c
        rl_recv, rl_done = scatter(
            rlow, lambda a, b, d, k: RL.at[a, b, d, k], c < kb, idx, spb * pair_count(z.C), True
        )
    for cp in locals_:
        cp.wait()
    arrive(rows_w)
    rows_p = []
    for dg in range(1, z.G):
        ss, rs = sems.next()
        cp = remote(ROWS.at[g], ROWS.at[g], ss, rs, ((g + dg) % z.G, r, c))
        rows_p.append((cp, ROWS.at[(g - dg + z.G) % z.G], rs))
    arrive(rr_w)
    rr_p = plane_send(z, lambda gg, xx: RR.at[core, gg, xx], sems)
    gl_recv()
    gl_p = plane_send(
        z, lambda gg, xx: GL.at[core, xx], sems, [(0, dx) for dx in range(1, z.X)]
    )
    if with_root:
        rl_recv()
        rl_p = plane_send(z, lambda gg, xx: RL.at[core, gg, xx], sems)
    arrive(rr_p)
    rr_c = core_send(z, lambda a: RR.at[a], sems)
    arrive(gl_p)
    gl_c = core_send(z, lambda a: GL.at[a], sems)
    pending = [rhs_w, rows_w, rr_w, rows_p, rr_p, gl_p, rr_c, gl_c]
    late = [rhs_w, rows_p, rr_c, gl_c]
    if with_root:
        arrive(rl_p)
        rl_c = core_send(z, lambda a: RL.at[a], sems)
        pending += [rl_p, rl_c]
        late += [rl_c]
    for w in late:
        arrive(w)
    for w in pending:
        sent(w)
    gl_done()
    if with_root:
        rl_done()


def gather_all(z, spb, with_root, glow, grhs, rows, rrhs, rlow):
    f32 = jnp.float32
    b1, n = grhs.shape
    ins = [glow, grhs, rows, rrhs] + ([rlow] if with_root else [])
    outs = [
        jax.ShapeDtypeStruct((CORES, z.X, pair_count(z.R), b1 // z.C, b1), f32),
        jax.ShapeDtypeStruct((z.R, b1, n), f32),
        jax.ShapeDtypeStruct((z.G, z.R, 1, b1), jnp.int32),
        jax.ShapeDtypeStruct((CORES, z.G, z.X, z.R) + rrhs.shape, f32),
    ]
    if with_root:
        s, span = rlow.shape
        outs.append(
            jax.ShapeDtypeStruct(
                (CORES, z.G, z.X, spb * pair_count(z.C), s // (z.G * z.C), span), f32
            )
        )
    n_in, n_out = len(ins), len(outs)
    n_sem = (
        4 * z.R + 2 * z.G * z.X + z.X + z.G + 4
        + max(pair_count(z.R), z.R * z.C) + max(spb * pair_count(z.C), z.G * z.R * z.C)
        + z.G * z.X
    )
    if not with_root:
        n_sem -= max(spb * pair_count(z.C), z.G * z.R * z.C)

    def body(*refs):
        gather_kernel(z, spb, with_root, refs[:n_in], refs[n_in : n_in + n_out], *refs[n_in + n_out :])

    return pl.pallas_call(
        body,
        out_shape=outs,
        in_specs=[pl.BlockSpec(memory_space=pl.ANY)] * n_in,
        out_specs=[pl.BlockSpec(memory_space=pl.ANY)] * n_out,
        scratch_shapes=[
            pltpu.SemaphoreType.DMA((n_sem,)),
            pltpu.SemaphoreType.DMA((n_sem,)),
            pltpu.SemaphoreType.DMA((3,)),
        ],
        compiler_params=pltpu.CompilerParams(collective_id=0, has_side_effects=True),
        name="gather_factors",
    )(*ins)


def update_kernel(z, part, out, got, total, send, recv, keep):
    g, r, c = here()
    x, core = c // CORES, c % CORES
    h = total.shape[0]
    sems = Sems(send, recv)
    greet(
        [(g, r, (c + d) % z.C) for d in range(1, z.C)]
        + [(g, (r + d) % z.R, c) for d in range(1, z.R)]
        + [((g + dg) % z.G, r, (x + dx) % z.X * CORES + core) for dg, dx in plane_offsets(z) if dg]
    )

    def chunk(k):
        return part.at[pl.ds(pl.multiple_of(k * h, 8), h)]

    own = pltpu.make_async_copy(chunk(c), got.at[c], keep.at[0])
    own.start()
    first = []
    for d in range(1, z.C):
        ss, rs = sems.next()
        t = (c + d) % z.C
        first.append((remote(chunk(t), got.at[c], ss, rs, (g, r, t)), got.at[(c - d + z.C) % z.C], rs))
    own.wait()
    arrive(first)
    acc = got[0]
    for k in range(1, z.C):
        acc = acc + got[k]
    total[...] = acc
    own = pltpu.make_async_copy(total, out.at[core, g, x, r], keep.at[0])
    own.start()
    second = row_send(z, total, lambda rr: out.at[core, g, x, rr], sems)
    own.wait()
    arrive(second)
    third = plane_send(z, lambda gg, xx: out.at[core, gg, xx], sems)
    arrive(third)
    fourth = core_send(z, lambda a: out.at[a], sems)
    arrive(fourth)
    for w in (first, second, third, fourth):
        sent(w)


def exchange_update(z, part):
    b1, n = part.shape
    h = b1 // z.C
    n_sem = z.C + z.R + z.G * z.X + 1
    return pl.pallas_call(
        functools.partial(update_kernel, z),
        out_shape=jax.ShapeDtypeStruct((CORES, z.G, z.X, z.R, h, n), jnp.float32),
        in_specs=[pl.BlockSpec(memory_space=pl.ANY)],
        out_specs=pl.BlockSpec(memory_space=pl.ANY),
        scratch_shapes=[
            pltpu.VMEM((z.C, h, n), jnp.float32),
            pltpu.VMEM((h, n), jnp.float32),
            pltpu.SemaphoreType.DMA((n_sem,)),
            pltpu.SemaphoreType.DMA((n_sem,)),
            pltpu.SemaphoreType.DMA((1,)),
        ],
        compiler_params=pltpu.CompilerParams(collective_id=1, has_side_effects=True),
        name="exchange_update",
    )(part)


def lifted_kernel(z, part, out, got, total, send, recv, keep):
    g, r, c = here()
    x, core = c // CORES, c % CORES
    h = total.shape[0]
    sems = Sems(send, recv)
    greet(
        [(g, (r + d) % z.R, c) for d in range(1, z.R)]
        + [(g, r, (x + dx) % z.X * CORES + core) for dx in range(1, z.X)]
        + [(g, r, x * CORES + 1 - core)]
    )

    def chunk(k):
        return part.at[pl.ds(pl.multiple_of(k * h, 8), h)]

    own = pltpu.make_async_copy(chunk(r), got.at[r], keep.at[0])
    own.start()
    first = []
    for d in range(1, z.R):
        ss, rs = sems.next()
        t = (r + d) % z.R
        first.append((remote(chunk(t), got.at[r], ss, rs, (g, t, c)), got.at[(r - d + z.R) % z.R], rs))
    own.wait()
    arrive(first)
    acc = got[0]
    for k in range(1, z.R):
        acc = acc + got[k]
    total[...] = acc
    own = pltpu.make_async_copy(total, out.at[core, x, r], keep.at[0])
    own.start()
    second = row_send(z, total, lambda rr: out.at[core, x, rr], sems)
    own.wait()
    arrive(second)
    third = plane_send(z, lambda gg, xx: out.at[core, xx], sems, [(0, dx) for dx in range(1, z.X)])
    arrive(third)
    fourth = core_send(z, lambda a: out.at[a], sems)
    arrive(fourth)
    for w in (first, second, third, fourth):
        sent(w)


def exchange_lifted(z, part):
    n, b1 = part.shape
    h = n // z.R
    n_sem = 2 * z.R + z.X + 1
    return pl.pallas_call(
        functools.partial(lifted_kernel, z),
        out_shape=jax.ShapeDtypeStruct((CORES, z.X, z.R, h, b1), jnp.float32),
        in_specs=[pl.BlockSpec(memory_space=pl.ANY)],
        out_specs=pl.BlockSpec(memory_space=pl.ANY),
        scratch_shapes=[
            pltpu.VMEM((z.R, h, b1), jnp.float32),
            pltpu.VMEM((h, b1), jnp.float32),
            pltpu.SemaphoreType.DMA((n_sem,)),
            pltpu.SemaphoreType.DMA((n_sem,)),
            pltpu.SemaphoreType.DMA((1,)),
        ],
        compiler_params=pltpu.CompilerParams(collective_id=2, has_side_effects=True),
        name="exchange_lifted",
    )(part)


def group_block(GL, k, j):
    idx = k * (k - 1) // 2 + j
    return jnp.concatenate([GL[q, idx] for q in range(GL.shape[0])], axis=0)


def forward_kernel(z, GL, GR, inv, off, y_ref, part_ref):
    b1 = inv.shape[1]
    ys = []
    for k in range(z.R):
        res = GR[k]
        for j in range(k):
            res = res - mm(group_block(GL, k, j), ys[j])
        ys.append(mm(inv[k * b1 : (k + 1) * b1], res))
        y_ref[k * b1 : (k + 1) * b1] = ys[k]
    c = lax.axis_index("col")
    own = y_ref[pl.ds(pl.multiple_of(c * b1, 8), b1)]
    part_ref[...] = mm(off[...], own)


def root_kernel(z, spb, UPD, ROWS, RR, RL, E, own_rows, off, x_ref, lift_ref, side, xt_ref):
    W0, span = E.shape
    p, n = RR.shape[-2:]
    h = UPD.shape[-2]
    b1 = h * z.C
    for g in range(z.G):
        for r in range(z.R):
            for c in range(z.C):
                at = ((g * z.R + r) * z.C + c) * p
                side[at : at + p] = RR[c % CORES, g, c // CORES, r]
    packed = []
    for g in range(z.G):
        u = jnp.concatenate(
            [UPD[c % CORES, g, c // CORES, r] for r in range(z.R) for c in range(z.C)], axis=0
        )
        packed.append(
            (
                jnp.concatenate(split(u), axis=1),
                jnp.concatenate([ROWS[g, r] for r in range(z.R)], axis=1),
            )
        )

    def block(k, j):
        pieces = []
        for s in range(spb):
            idx = spb * (k * (k - 1) // 2) + s * k + j
            pieces += [RL[q, idx] for q in range(RL.shape[0])]
        return jnp.concatenate(pieces, axis=0)

    ys = []
    for k in range(z.C):
        res = side[k * span : (k + 1) * span]
        for w, rows in packed:
            ids = lax.broadcasted_iota(jnp.int32, (span, rows.shape[1]), 0) + k * span
            hot = jnp.where(ids == rows, 1.0, 0.0).astype(jnp.bfloat16)
            both = bdot(hot, w)
            res = res - (both[:, :n] + both[:, n:])
        for j in range(k):
            res = res - mm(block(k, j), ys[j])
        ys.append(mm(E[k * span : (k + 1) * span], res))
    xs = [None] * z.C
    for k in reversed(range(z.C)):
        res = ys[k].T
        for i in range(k + 1, z.C):
            res = res - tmm(xs[i], block(i, k))
        xs[k] = tmm(res, E[k * span : (k + 1) * span])
        side[k * span : (k + 1) * span] = xs[k].T
    g, r, c = here()
    flat = (g * z.R + r) * z.C + c
    x_ref[...] = side[pl.ds(flat * p, p)]
    picked = jnp.zeros((n, b1), jnp.float32)
    for k in range(z.C):
        ids = lax.broadcasted_iota(jnp.int32, (span, b1), 0) + k * span
        hot = jnp.where(ids == own_rows[...], 1.0, 0.0).astype(jnp.bfloat16)
        both = bdot(jnp.concatenate(split(xs[k]), axis=0), hot)
        picked = picked + both[:n] + both[n:]
    lift_ref[...] = tmm(picked, off[...])


def backward_kernel(z, GL, inv, y_ref, lift, out_ref, xs_ref):
    b1 = inv.shape[1]
    xs = [None] * z.R
    for k in reversed(range(z.R)):
        lk = jnp.concatenate([lift[k % CORES, k // CORES, r] for r in range(z.R)], axis=0)
        res = y_ref[k * b1 : (k + 1) * b1].T - lk
        for i in range(k + 1, z.R):
            res = res - tmm(xs[i], group_block(GL, i, k))
        xs[k] = tmm(res, inv[k * b1 : (k + 1) * b1])
        xs_ref[k * b1 : (k + 1) * b1] = xs[k].T
    r = lax.axis_index("row")
    out_ref[...] = xs_ref[pl.ds(pl.multiple_of(r * b1, 8), b1)]


def on_chip(body, out_shape, scratch, name, *args):
    return pl.pallas_call(
        body,
        out_shape=out_shape,
        scratch_shapes=scratch,
        compiler_params=pltpu.CompilerParams(vmem_limit_bytes=VMEM_BYTES),
        name=name,
    )(*args)


def local(z, group_rhs, group_lower, group_diag_inv, group_offdiag, group_rows, root_rhs, root_lower, root_diag_inv):
    f32 = jnp.float32
    b1, n = group_rhs.shape[1:]
    width = group_diag_inv.shape[1]
    W0, span = root_diag_inv.shape
    strip = root_lower.shape[0]
    spb = span // strip
    inv, off = group_diag_inv[0], group_offdiag[0]
    with_root = strip % (8 * z.G * z.C) == 0
    got = gather_all(z, spb, with_root, group_lower[0], group_rhs[0], group_rows, root_rhs, root_lower)
    GL, GR, ROWS, RR = got[:4]
    if with_root:
        RL = got[4].reshape((z.G * z.C,) + got[4].shape[3:])
    else:
        whole = lax.all_gather(root_lower, ("grp", "row", "col"))
        whole = whole.reshape(z.G * z.R, z.C, strip, span)
        RL = jnp.stack(
            [whole[k * spb + s, j] for k in range(z.C) for s in range(spb) for j in range(k)]
        )[None]
    GL = GL.reshape((z.C,) + GL.shape[2:])
    y, part = on_chip(
        functools.partial(forward_kernel, z),
        [jax.ShapeDtypeStruct((width, n), f32), jax.ShapeDtypeStruct((b1, n), f32)],
        [], "group_forward", GL, GR, inv, off,
    )
    UPD = exchange_update(z, part)
    root_x, lift = on_chip(
        functools.partial(root_kernel, z, spb),
        [jax.ShapeDtypeStruct(root_rhs.shape, f32), jax.ShapeDtypeStruct((n, b1), f32)],
        [pltpu.VMEM((W0, n), f32), pltpu.VMEM((n, W0), f32)],
        "root_solve", UPD, ROWS, RR, RL, root_diag_inv, group_rows, off,
    )
    lifted = exchange_lifted(z, lift)
    out = on_chip(
        functools.partial(backward_kernel, z),
        jax.ShapeDtypeStruct((b1, n), f32),
        [pltpu.VMEM((width, n), f32)],
        "group_backward", GL, inv, y, lifted,
    )
    return out[None], root_x


def solution(mesh):
    z = Sizes(mesh.shape)
    placed = (
        P("grp", "row", None),
        P("grp", "row", "col"),
        P("grp", None, None),
        P("grp", "row", "col"),
        P("grp", "row"),
        P(("grp", "row", "col"), None),
        P(("grp", "row"), "col"),
        P(),
    )
    return jax.shard_map(
        functools.partial(local, z),
        mesh=mesh,
        in_specs=placed,
        out_specs=(P("grp", "row", None), P(("grp", "row", "col"), None)),
        check_vma=False,
    )
```

time: 1690 us -> 196 us (0.12)
  waiting for transfers between devices: 1590 us -> 0 us
  Pallas kernels: 0 us -> 195 us
  matrix products: 55.5 us -> 0 us
  local copies, waits for them, and re-layouts: 20.9 us -> 0 us
    psum x15 -> x0, waiting for transfers between devices: 1590 us -> none  [the longest x7 884 us: local(): summed = lax.psum(contrib, ('grp', 'row', 'col'))]
    pallas_call x0 -> x6, Pallas kernels: none -> 195 us  [the longest x1 118 us: gather_all(): pl.pallas_call(body, out_shape=outs, in_specs=[pl.BlockSpec(memory_space=...]
    dot_general x34 -> x0, matrix products: 55.5 us -> none  [the longest x17 27.9 us: exact_dot(): jnp.dot(left, right, precision=lax.Precision.HIGHEST, preferred_element_t...]
  transfers between devices with their start and end apart: 15 -> 0, of which waited for: 15 -> 0; matrix products, arithmetic and copies ran while one was open for 1% -> 0% of each run, Pallas kernels for 0% -> 0%
where the time goes in v1:
time: 196 us
  Pallas kernels  195 us (99%)
    pallas_call x1, Pallas kernels, gather_all(): pl.pallas_call(body, out_shape=outs, in_specs=[pl.BlockSpec(memory_space=...  118 us
    pallas_call x1, Pallas kernels, exchange_update(): pl.pallas_call(functools.partial(update_kernel, z), out_shape=jax.ShapeDt...  33.7 us
    pallas_call x3, Pallas kernels, on_chip(): pl.pallas_call(body, out_shape=out_shape, scratch_shapes=scratch, compile...  25 us
    pallas_call x1, Pallas kernels, exchange_lifted(): pl.pallas_call(functools.partial(lifted_kernel, z), out_shape=jax.ShapeDt...  18.5 us

profile of v1, /device:TPU:0, one launch (start us, length us, event | category | flops | bytes accessed | tf_op | source)
XLA Modules:
  0.0 195.9 jit_solution(11305444422958636676)
XLA Ops:
  0.6 118.2 %gather_factors.1 = (f32[2,2,6,64,256]{4,3,2,1,0:T(8,128)}, f32[4,256,128]{2,1,0:T(8,128)}, s32[2,4,1,256]{3,2,1,0:T(1,128)}, f32[2,2,2,4,64,128]{5,4,3,2,1,0:T(8,128)}, f32[2,2,2,12,32,512]{5,4,3,2,1,0:T(8,128)}) custom-call(f32[256,256]{1,0:T(8,128)} %bitcast.14, f32[256,128]{1,0:T(8,128)} %bitcast.15, s32[1,256]{1,0:T(1,128)} %own_rows.1, ...), custom_call_target="tpu_custom_call" | custom-call | tf_op jit(solution)/shard_map/gather_factors/pallas_call | solution.py:281
  118.8 4.6 %group_forward.1 = (f32[1024,128]{1,0:T(8,128)}, f32[256,128]{1,0:T(8,128)}) custom-call(f32[4,6,64,256]{3,2,1,0:T(8,128)} %bitcast.8, f32[4,256,128]{2,1,0:T(8,128)} %get-tuple-element.12.GR, f32[1024,256]{1,0:T(8,128)} %bitcast.10, f32[256,256]{1,0:T(8,128)} %bitcast.12), custom_call_target="tpu_custom_call" | custom-call | tf_op jit(solution)/shard_map/group_forward/pallas_call | solution.py:511
  123.4 33.7 %exchange_update.1.UPD = f32[2,2,2,4,64,128]{5,4,3,2,1,0:T(8,128)} custom-call(f32[256,128]{1,0:T(8,128)} %get-tuple-element.14.part), custom_call_target="tpu_custom_call" | custom-call | tf_op jit(solution)/shard_map/exchange_update/pallas_call | solution.py:340
  157.1 15.8 %root_solve.1 = (f32[64,128]{1,0:T(8,128)}, f32[128,256]{1,0:T(8,128)}) custom-call(f32[2,2,2,4,64,128]{5,4,3,2,1,0:T(8,128)} %exchange_update.1.UPD, s32[2,4,1,256]{3,2,1,0:T(1,128)} %get-tuple-element.15.ROWS, f32[2,2,2,4,64,128]{5,4,3,2,1,0:T(8,128)} %get-tuple-element.16.RR, f32[8,12,32,512]{3,2,1,0:T(8,128)} %bitcast.7, f32[2048,512]{1,0:T(8,128)} %E.1, ...), custom_call_target="tpu_custom_call" | custom-call | tf_op jit(solution)/shard_map/root_solve/pallas_call | solution.py:511
  172.9 18.5 %exchange_lifted.1.lift = f32[2,2,4,32,256]{4,3,2,1,0:T(8,128)} custom-call(f32[128,256]{1,0:T(8,128)} %get-tuple-element.18.part), custom_call_target="tpu_custom_call" | custom-call | tf_op jit(solution)/shard_map/exchange_lifted/pallas_call | solution.py:401
  191.4 4.5 %group_backward.1 = f32[256,128]{1,0:T(8,128)} custom-call(f32[4,6,64,256]{3,2,1,0:T(8,128)} %bitcast.9, f32[1024,256]{1,0:T(8,128)} %bitcast.11, f32[1024,128]{1,0:T(8,128)} %get-tuple-element.13.y_ref, f32[2,2,4,32,256]{4,3,2,1,0:T(8,128)} %exchange_lifted.1.lift), custom_call_target="tpu_custom_call" | custom-call | tf_op jit(solution)/shard_map/group_backward/pallas_call | solution.py:511

commit v2 on v1

--- a/solution.py
+++ b/solution.py
@@ -75,6 +75,10 @@
         k = self.at
         self.at += 1
         return self.send.at[k], self.recv.at[k]
+
+    def block(self, n):
+        self.at += n
+        return self.at - n
 
 
 def plane_offsets(z):
@@ -126,28 +130,135 @@
     return n * (n - 1) // 2
 
 
+class Pieces:
+    def __init__(self, z, src, slot, held, index, count, groups, forward, sems):
+        self.z, self.src, self.slot, self.held, self.index = z, src, slot, held, index
+        self.count, self.groups, self.forward = count, groups, forward
+        g = lax.axis_index("grp")
+        self.gs = range(z.G) if groups else (g,)
+        self.sources = [(gs, cs) for gs in self.gs for cs in range(z.C)]
+        self.plane = [(dg, dc) for dg in (range(z.G) if groups else (0,)) for dc in range(z.C)]
+        self.offs = plane_offsets(z) if forward else []
+        ns, no = len(self.sources), len(self.offs)
+        self.send, self.recv = sems.send, sems.recv
+        self.b_recv = sems.block(count)
+        self.b_first = sems.block(len(self.plane))
+        self.b_row = sems.block(ns * z.R)
+        self.b_on = sems.block(ns * z.R * no)
+        self.b_on_recv = sems.block(no * count)
+
+    def mine(self, k):
+        g, r, c = here()
+        return self.slot(c % CORES, g, c // CORES, k)
+
+    def copies(self, start):
+        z = self.z
+        g, r, c = here()
+        k = self.index(g, r, c)
+        rows_each = self.slot(0, 0, 0, 0).shape[0]
+
+        @pl.when(self.held(g, r, c))
+        def _():
+            for m, (dg, dc) in enumerate(self.plane):
+                tg, tc = (g + dg) % z.G, (c + dc) % z.C
+                tx, tcore = tc // CORES, tc % CORES
+                q = (tcore * z.G + tg) * z.X + tx if self.groups else tcore * z.X + tx
+                chunk = self.src.at[pl.ds(pl.multiple_of(q * rows_each, 8), rows_each)]
+                dst, rs = self.slot(tcore, tg, tx, k), self.recv.at[self.b_recv + k]
+                if dg or dc:
+                    cp = pltpu.make_async_remote_copy(
+                        src_ref=chunk, dst_ref=dst, send_sem=self.send.at[self.b_first + m],
+                        recv_sem=rs, device_id=(tg, r, tc), device_id_type=MESH,
+                    )
+                    cp.start() if start else cp.wait_send()
+                elif start:
+                    pltpu.make_async_copy(chunk, dst, rs).start()
+
+    def onward(self, d, start):
+        z = self.z
+        g, r, c = here()
+        x, core = c // CORES, c % CORES
+        rs = (r - d + z.R) % z.R
+        for m, (gs, cs) in enumerate(self.sources):
+            k = self.index(gs, rs, cs)
+
+            @pl.when(self.held(gs, rs, cs))
+            def _():
+                if start:
+                    wait_on(self.mine(k), self.recv.at[self.b_recv + k])
+                targets = []
+                if d == 0:
+                    for e in range(1, z.R):
+                        targets.append(
+                            ((g, (r + e) % z.R, c), self.b_row + m * z.R + e, self.b_recv + k)
+                        )
+                for o, (dg, dx) in enumerate(self.offs):
+                    targets.append(
+                        (
+                            ((g + dg) % z.G, r, (x + dx) % z.X * CORES + core),
+                            self.b_on + (d * len(self.sources) + m) * len(self.offs) + o,
+                            self.b_on_recv + o * self.count + k,
+                        )
+                    )
+                for dev, si, ri in targets:
+                    cp = pltpu.make_async_remote_copy(
+                        src_ref=self.mine(k), dst_ref=self.mine(k), send_sem=self.send.at[si],
+                        recv_sem=self.recv.at[ri], device_id=dev, device_id_type=MESH,
+                    )
+                    cp.start() if start else cp.wait_send()
+
+    def plane_arrived(self, o):
+        z = self.z
+        g, r, c = here()
+        x, core = c // CORES, c % CORES
+        dg, dx = self.offs[o]
+        fg, fx = (g - dg + z.G) % z.G, (x - dx + z.X) % z.X
+        for k in range(self.count):
+            wait_on(self.slot(core, fg, fx, k), self.recv.at[self.b_on_recv + o * self.count + k])
+        return fg, fx
+
+    def finish(self):
+        self.copies(False)
+        for d in range(self.z.R):
+            self.onward(d, False)
+
+
 def gather_kernel(z, spb, with_root, refs_in, refs_out, send, recv, keep):
     g, r, c = here()
     x, core = c // CORES, c % CORES
     glow, grhs, rows, rrhs = refs_in[:4]
     GL, GR, ROWS, RR = refs_out[:4]
     sems = Sems(send, recv)
-    if with_root:
-        devs = [
-            ((g + dg) % z.G, (r + dr) % z.R, (c + dc) % z.C)
-            for dg in range(z.G) for dr in range(z.R) for dc in range(z.C) if dg or dr or dc
-        ]
-    else:
-        devs = [
-            (g, (r + dr) % z.R, (c + dc) % z.C)
-            for dr in range(z.R) for dc in range(z.C) if dr or dc
-        ]
+    groups = range(z.G) if with_root else (0,)
+    devs = [
+        ((g + dg) % z.G, r, (c + dc) % z.C) for dg in groups for dc in range(z.C) if dg or dc
+    ] + [(g, (r + d) % z.R, c) for d in range(1, z.R)]
+    if not with_root:
         devs += [
             ((g + dg) % z.G, r, (x + dx) % z.X * CORES + core)
             for dg, dx in plane_offsets(z) if dg
         ]
     greet(devs)
 
+    low = Pieces(
+        z, glow, lambda a, b, d, k: GL.at[a, d, k], lambda gg, rr, cc: cc < rr,
+        lambda gg, rr, cc: rr * (rr - 1) // 2 + cc, pair_count(z.R), False, False, sems,
+    )
+    low.copies(True)
+    if with_root:
+        rlow, RL = refs_in[4], refs_out[4]
+
+        def index(gg, rr, cc):
+            strip = gg * z.R + rr
+            kb = strip // spb
+            return spb * (kb * (kb - 1) // 2) + (strip - kb * spb) * kb + cc
+
+        root = Pieces(
+            z, rlow, lambda a, b, d, k: RL.at[a, b, d, k],
+            lambda gg, rr, cc: cc < (gg * z.R + rr) // spb,
+            index, spb * pair_count(z.C), True, True, sems,
+        )
+        root.copies(True)
     locals_ = []
     for k, (src, dst) in enumerate(
         ((grhs, GR.at[r]), (rows, ROWS.at[g, r]), (rrhs, RR.at[core, g, x, r]))
@@ -155,63 +266,12 @@
         cp = pltpu.make_async_copy(src, dst, keep.at[k])
         cp.start()
         locals_.append(cp)
-
-    def scatter(src, out_slot, holder, idx, n_pieces, groups):
-        base = sems.at
-        rows_each = out_slot(0, 0, 0, 0).shape[0]
-        offs = [
-            (dg, dr, dc)
-            for dg in (range(z.G) if groups else (0,)) for dr in range(z.R) for dc in range(z.C)
-        ]
-        sems.at += max(n_pieces, len(offs))
-
-        def chunk(tg, tc):
-            tx, tcore = tc // CORES, tc % CORES
-            q = (tcore * z.G + tg) * z.X + tx if groups else tcore * z.X + tx
-            return src.at[pl.ds(pl.multiple_of(q * rows_each, 8), rows_each)]
-
-        def copies(start):
-            for k, (dg, dr, dc) in enumerate(offs):
-                tg, tr, tc = (g + dg) % z.G, (r + dr) % z.R, (c + dc) % z.C
-                dst = out_slot(tc % CORES, tg, tc // CORES, idx)
-                if dg or dr or dc:
-                    cp = pltpu.make_async_remote_copy(
-                        src_ref=chunk(tg, tc), dst_ref=dst, send_sem=send.at[base + k],
-                        recv_sem=recv.at[base + idx], device_id=(tg, tr, tc), device_id_type=MESH,
-                    )
-                    cp.start() if start else cp.wait_send()
-                elif start:
-                    pltpu.make_async_copy(chunk(tg, tc), dst, recv.at[base + idx]).start()
-
-        @pl.when(holder)
-        def _():
-            copies(True)
-
-        def received():
-            for k in range(n_pieces):
-                wait_on(out_slot(core, g, x, k), recv.at[base + k])
-
-        def done():
-            @pl.when(holder)
-            def _():
-                copies(False)
-
-        return received, done
-
     rhs_w = row_send(z, grhs, lambda rr: GR.at[rr], sems)
     rows_w = row_send(z, rows, lambda rr: ROWS.at[g, rr], sems)
     rr_w = row_send(z, rrhs, lambda rr: RR.at[core, g, x, rr], sems)
-    gl_recv, gl_done = scatter(
-        glow, lambda a, b, d, k: GL.at[a, d, k], c < r, r * (r - 1) // 2 + c, pair_count(z.R), False
-    )
-    if with_root:
-        rlow, RL = refs_in[4], refs_out[4]
-        strip = g * z.R + r
-        kb = strip // spb
-        idx = spb * (kb * (kb - 1) // 2) + (strip - kb * spb) * kb + c
-        rl_recv, rl_done = scatter(
-            rlow, lambda a, b, d, k: RL.at[a, b, d, k], c < kb, idx, spb * pair_count(z.C), True
-        )
+    low.onward(0, True)
+    if with_root:
+        root.onward(0, True)
     for cp in locals_:
         cp.wait()
     arrive(rows_w)
@@ -222,13 +282,14 @@
         rows_p.append((cp, ROWS.at[(g - dg + z.G) % z.G], rs))
     arrive(rr_w)
     rr_p = plane_send(z, lambda gg, xx: RR.at[core, gg, xx], sems)
-    gl_recv()
+    for d in range(1, z.R):
+        low.onward(d, True)
     gl_p = plane_send(
         z, lambda gg, xx: GL.at[core, xx], sems, [(0, dx) for dx in range(1, z.X)]
     )
     if with_root:
-        rl_recv()
-        rl_p = plane_send(z, lambda gg, xx: RL.at[core, gg, xx], sems)
+        for d in range(1, z.R):
+            root.onward(d, True)
     arrive(rr_p)
     rr_c = core_send(z, lambda a: RR.at[a], sems)
     arrive(gl_p)
@@ -236,17 +297,19 @@
     pending = [rhs_w, rows_w, rr_w, rows_p, rr_p, gl_p, rr_c, gl_c]
     late = [rhs_w, rows_p, rr_c, gl_c]
     if with_root:
-        arrive(rl_p)
-        rl_c = core_send(z, lambda a: RL.at[a], sems)
-        pending += [rl_p, rl_c]
+        rl_c = core_send(z, lambda a: RL.at[a, g, x], sems)
+        for o in range(len(root.offs)):
+            fg, fx = root.plane_arrived(o)
+            rl_c += core_send(z, lambda a: RL.at[a, fg, fx], sems)
+        pending += [rl_c]
         late += [rl_c]
     for w in late:
         arrive(w)
     for w in pending:
         sent(w)
-    gl_done()
-    if with_root:
-        rl_done()
+    low.finish()
+    if with_root:
+        root.finish()
 
 
 def gather_all(z, spb, with_root, glow, grhs, rows, rrhs, rlow):
@@ -267,13 +330,11 @@
             )
         )
     n_in, n_out = len(ins), len(outs)
-    n_sem = (
-        4 * z.R + 2 * z.G * z.X + z.X + z.G + 4
-        + max(pair_count(z.R), z.R * z.C) + max(spb * pair_count(z.C), z.G * z.R * z.C)
-        + z.G * z.X
-    )
-    if not with_root:
-        n_sem -= max(spb * pair_count(z.C), z.G * z.R * z.C)
+    n_sem = 4 * z.R + 2 * z.G * z.X + z.X + z.G + 4
+    n_sem += pair_count(z.R) + z.C + z.C * z.R
+    if with_root:
+        count, ns, no = spb * pair_count(z.C), z.G * z.C, z.G * z.X - 1
+        n_sem += count + ns + ns * z.R + ns * z.R * no + no * count + z.G * z.X
 
     def body(*refs):
         gather_kernel(z, spb, with_root, refs[:n_in], refs[n_in : n_in + n_out], *refs[n_in + n_out :])

time: 196 us -> 154 us (0.79)
  Pallas kernels: 195 us -> 153 us
    pallas_call x1, Pallas kernels: 118 us -> 86.4 us  [gather_all(): pl.pallas_call(body, out_shape=outs, in_specs=[pl.BlockSpec(memory_space=...]
    pallas_call x1, Pallas kernels: 33.7 us -> 23 us  [exchange_update(): pl.pallas_call(functools.partial(update_kernel, z), out_shape=jax.ShapeDt...]
where the time goes in v2:
time: 154 us; the launch traced here: 153 us
  Pallas kernels  153 us (99%)
    pallas_call x1, Pallas kernels, gather_all(): pl.pallas_call(body, out_shape=outs, in_specs=[pl.BlockSpec(memory_space=...  86.4 us
    pallas_call x3, Pallas kernels, on_chip(): pl.pallas_call(body, out_shape=out_shape, scratch_shapes=scratch, compile...  25 us
    pallas_call x1, Pallas kernels, exchange_update(): pl.pallas_call(functools.partial(update_kernel, z), out_shape=jax.ShapeDt...  23 us
    pallas_call x1, Pallas kernels, exchange_lifted(): pl.pallas_call(functools.partial(lifted_kernel, z), out_shape=jax.ShapeDt...  18.4 us

profile of v2, /device:TPU:0, one launch (start us, length us, event | category | flops | bytes accessed | tf_op | source)
XLA Modules:
  0.0 153.4 jit_solution(16737726699596066422)
XLA Ops:
  0.6 86.4 %gather_factors.1 = (f32[2,2,6,64,256]{4,3,2,1,0:T(8,128)}, f32[4,256,128]{2,1,0:T(8,128)}, s32[2,4,1,256]{3,2,1,0:T(1,128)}, f32[2,2,2,4,64,128]{5,4,3,2,1,0:T(8,128)}, f32[2,2,2,12,32,512]{5,4,3,2,1,0:T(8,128)}) custom-call(f32[256,256]{1,0:T(8,128)} %bitcast.14, f32[256,128]{1,0:T(8,128)} %bitcast.15, s32[1,256]{1,0:T(1,128)} %own_rows.1, ...), custom_call_target="tpu_custom_call" | custom-call | tf_op jit(solution)/shard_map/gather_factors/pallas_call | solution.py:342
  87.1 4.6 %group_forward.1 = (f32[1024,128]{1,0:T(8,128)}, f32[256,128]{1,0:T(8,128)}) custom-call(f32[4,6,64,256]{3,2,1,0:T(8,128)} %bitcast.8, f32[4,256,128]{2,1,0:T(8,128)} %get-tuple-element.12.GR, f32[1024,256]{1,0:T(8,128)} %bitcast.10, f32[256,256]{1,0:T(8,128)} %bitcast.12), custom_call_target="tpu_custom_call" | custom-call | tf_op jit(solution)/shard_map/group_forward/pallas_call | solution.py:572
  91.7 23.0 %exchange_update.1.UPD = f32[2,2,2,4,64,128]{5,4,3,2,1,0:T(8,128)} custom-call(f32[256,128]{1,0:T(8,128)} %get-tuple-element.14.part), custom_call_target="tpu_custom_call" | custom-call | tf_op jit(solution)/shard_map/exchange_update/pallas_call | solution.py:401
  114.7 15.8 %root_solve.1 = (f32[64,128]{1,0:T(8,128)}, f32[128,256]{1,0:T(8,128)}) custom-call(f32[2,2,2,4,64,128]{5,4,3,2,1,0:T(8,128)} %exchange_update.1.UPD, s32[2,4,1,256]{3,2,1,0:T(1,128)} %get-tuple-element.15.ROWS, f32[2,2,2,4,64,128]{5,4,3,2,1,0:T(8,128)} %get-tuple-element.16.RR, f32[8,12,32,512]{3,2,1,0:T(8,128)} %bitcast.7, f32[2048,512]{1,0:T(8,128)} %E.1, ...), custom_call_target="tpu_custom_call" | custom-call | tf_op jit(solution)/shard_map/root_solve/pallas_call | solution.py:572
  130.5 18.4 %exchange_lifted.1.lift = f32[2,2,4,32,256]{4,3,2,1,0:T(8,128)} custom-call(f32[128,256]{1,0:T(8,128)} %get-tuple-element.18.part), custom_call_target="tpu_custom_call" | custom-call | tf_op jit(solution)/shard_map/exchange_lifted/pallas_call | solution.py:462
  148.8 4.5 %group_backward.1 = f32[256,128]{1,0:T(8,128)} custom-call(f32[4,6,64,256]{3,2,1,0:T(8,128)} %bitcast.9, f32[1024,256]{1,0:T(8,128)} %bitcast.11, f32[1024,128]{1,0:T(8,128)} %get-tuple-element.13.y_ref, f32[2,2,4,32,256]{4,3,2,1,0:T(8,128)} %exchange_lifted.1.lift), custom_call_target="tpu_custom_call" | custom-call | tf_op jit(solution)/shard_map/group_backward/pallas_call | solution.py:572

commit v3 on v2

--- a/solution.py
+++ b/solution.py
@@ -223,11 +223,11 @@
             self.onward(d, False)
 
 
-def gather_kernel(z, spb, with_root, refs_in, refs_out, send, recv, keep):
+def gather_kernel(z, spb, with_root, refs_in, refs_out, GL, GR, part, got, total, send, recv, keep):
     g, r, c = here()
     x, core = c // CORES, c % CORES
-    glow, grhs, rows, rrhs = refs_in[:4]
-    GL, GR, ROWS, RR = refs_out[:4]
+    glow, grhs, rows, rrhs, inv, off = refs_in[:6]
+    GL_out, ROWS, RR, y_ref, UPD = refs_out[:5]
     sems = Sems(send, recv)
     groups = range(z.G) if with_root else (0,)
     devs = [
@@ -246,7 +246,7 @@
     )
     low.copies(True)
     if with_root:
-        rlow, RL = refs_in[4], refs_out[4]
+        rlow, RL = refs_in[6], refs_out[5]
 
         def index(gg, rr, cc):
             strip = gg * z.R + rr
@@ -295,75 +295,16 @@
     arrive(gl_p)
     gl_c = core_send(z, lambda a: GL.at[a], sems)
     pending = [rhs_w, rows_w, rr_w, rows_p, rr_p, gl_p, rr_c, gl_c]
-    late = [rhs_w, rows_p, rr_c, gl_c]
+    late = [rows_p, rr_c]
     if with_root:
         rl_c = core_send(z, lambda a: RL.at[a, g, x], sems)
-        for o in range(len(root.offs)):
-            fg, fx = root.plane_arrived(o)
-            rl_c += core_send(z, lambda a: RL.at[a, fg, fx], sems)
-        pending += [rl_c]
-        late += [rl_c]
-    for w in late:
-        arrive(w)
-    for w in pending:
-        sent(w)
-    low.finish()
-    if with_root:
-        root.finish()
-
-
-def gather_all(z, spb, with_root, glow, grhs, rows, rrhs, rlow):
-    f32 = jnp.float32
-    b1, n = grhs.shape
-    ins = [glow, grhs, rows, rrhs] + ([rlow] if with_root else [])
-    outs = [
-        jax.ShapeDtypeStruct((CORES, z.X, pair_count(z.R), b1 // z.C, b1), f32),
-        jax.ShapeDtypeStruct((z.R, b1, n), f32),
-        jax.ShapeDtypeStruct((z.G, z.R, 1, b1), jnp.int32),
-        jax.ShapeDtypeStruct((CORES, z.G, z.X, z.R) + rrhs.shape, f32),
-    ]
-    if with_root:
-        s, span = rlow.shape
-        outs.append(
-            jax.ShapeDtypeStruct(
-                (CORES, z.G, z.X, spb * pair_count(z.C), s // (z.G * z.C), span), f32
-            )
-        )
-    n_in, n_out = len(ins), len(outs)
-    n_sem = 4 * z.R + 2 * z.G * z.X + z.X + z.G + 4
-    n_sem += pair_count(z.R) + z.C + z.C * z.R
-    if with_root:
-        count, ns, no = spb * pair_count(z.C), z.G * z.C, z.G * z.X - 1
-        n_sem += count + ns + ns * z.R + ns * z.R * no + no * count + z.G * z.X
-
-    def body(*refs):
-        gather_kernel(z, spb, with_root, refs[:n_in], refs[n_in : n_in + n_out], *refs[n_in + n_out :])
-
-    return pl.pallas_call(
-        body,
-        out_shape=outs,
-        in_specs=[pl.BlockSpec(memory_space=pl.ANY)] * n_in,
-        out_specs=[pl.BlockSpec(memory_space=pl.ANY)] * n_out,
-        scratch_shapes=[
-            pltpu.SemaphoreType.DMA((n_sem,)),
-            pltpu.SemaphoreType.DMA((n_sem,)),
-            pltpu.SemaphoreType.DMA((3,)),
-        ],
-        compiler_params=pltpu.CompilerParams(collective_id=0, has_side_effects=True),
-        name="gather_factors",
-    )(*ins)
-
-
-def update_kernel(z, part, out, got, total, send, recv, keep):
-    g, r, c = here()
-    x, core = c // CORES, c % CORES
+    arrive(rhs_w)
+    arrive(gl_c)
+    copy_out = pltpu.make_async_copy(GL, GL_out, keep.at[3])
+    copy_out.start()
+    forward(z, GL, GR, inv, off, y_ref, part)
+
     h = total.shape[0]
-    sems = Sems(send, recv)
-    greet(
-        [(g, r, (c + d) % z.C) for d in range(1, z.C)]
-        + [(g, (r + d) % z.R, c) for d in range(1, z.R)]
-        + [((g + dg) % z.G, r, (x + dx) % z.X * CORES + core) for dg, dx in plane_offsets(z) if dg]
-    )
 
     def chunk(k):
         return part.at[pl.ds(pl.multiple_of(k * h, 8), h)]
@@ -381,38 +322,84 @@
     for k in range(1, z.C):
         acc = acc + got[k]
     total[...] = acc
-    own = pltpu.make_async_copy(total, out.at[core, g, x, r], keep.at[0])
+    own = pltpu.make_async_copy(total, UPD.at[core, g, x, r], keep.at[0])
     own.start()
-    second = row_send(z, total, lambda rr: out.at[core, g, x, rr], sems)
+    second = row_send(z, total, lambda rr: UPD.at[core, g, x, rr], sems)
     own.wait()
     arrive(second)
-    third = plane_send(z, lambda gg, xx: out.at[core, gg, xx], sems)
+    third = plane_send(z, lambda gg, xx: UPD.at[core, gg, xx], sems)
+    if with_root:
+        for o in range(len(root.offs)):
+            fg, fx = root.plane_arrived(o)
+            rl_c += core_send(z, lambda a: RL.at[a, fg, fx], sems)
+        pending += [rl_c]
+        late += [rl_c]
     arrive(third)
-    fourth = core_send(z, lambda a: out.at[a], sems)
-    arrive(fourth)
-    for w in (first, second, third, fourth):
+    fourth = core_send(z, lambda a: UPD.at[a], sems)
+    late += [fourth]
+    pending += [first, second, third, fourth]
+    for w in late:
+        arrive(w)
+    for w in pending:
         sent(w)
-
-
-def exchange_update(z, part):
-    b1, n = part.shape
-    h = b1 // z.C
-    n_sem = z.C + z.R + z.G * z.X + 1
+    copy_out.wait()
+    low.finish()
+    if with_root:
+        root.finish()
+
+
+def gather_all(z, spb, with_root, glow, grhs, rows, rrhs, inv, off, rlow):
+    f32 = jnp.float32
+    b1, n = grhs.shape
+    ins = [glow, grhs, rows, rrhs, inv, off] + ([rlow] if with_root else [])
+    outs = [
+        jax.ShapeDtypeStruct((CORES, z.X, pair_count(z.R), b1 // z.C, b1), f32),
+        jax.ShapeDtypeStruct((z.G, z.R, 1, b1), jnp.int32),
+        jax.ShapeDtypeStruct((CORES, z.G, z.X, z.R) + rrhs.shape, f32),
+        jax.ShapeDtypeStruct((z.R * b1, n), f32),
+        jax.ShapeDtypeStruct((CORES, z.G, z.X, z.R, b1 // z.C, n), f32),
+    ]
+    if with_root:
+        s, span = rlow.shape
+        outs.append(
+            jax.ShapeDtypeStruct(
+                (CORES, z.G, z.X, spb * pair_count(z.C), s // (z.G * z.C), span), f32
+            )
+        )
+    n_in, n_out = len(ins), len(outs)
+    n_sem = 5 * z.R + 3 * z.G * z.X + z.X + z.G + z.C + 5
+    n_sem += pair_count(z.R) + z.C + z.C * z.R
+    if with_root:
+        count, ns, no = spb * pair_count(z.C), z.G * z.C, z.G * z.X - 1
+        n_sem += count + ns + ns * z.R + ns * z.R * no + no * count + z.G * z.X
+
+    def body(*refs):
+        gather_kernel(z, spb, with_root, refs[:n_in], refs[n_in : n_in + n_out], *refs[n_in + n_out :])
+
     return pl.pallas_call(
-        functools.partial(update_kernel, z),
-        out_shape=jax.ShapeDtypeStruct((CORES, z.G, z.X, z.R, h, n), jnp.float32),
-        in_specs=[pl.BlockSpec(memory_space=pl.ANY)],
-        out_specs=pl.BlockSpec(memory_space=pl.ANY),
+        body,
+        out_shape=outs,
+        in_specs=[
+            pl.BlockSpec(memory_space=pltpu.VMEM if k in (4, 5) else pl.ANY) for k in range(n_in)
+        ],
+        out_specs=[
+            pl.BlockSpec(memory_space=pltpu.VMEM if k == 3 else pl.ANY) for k in range(n_out)
+        ],
         scratch_shapes=[
-            pltpu.VMEM((z.C, h, n), jnp.float32),
-            pltpu.VMEM((h, n), jnp.float32),
+            pltpu.VMEM(outs[0].shape, f32),
+            pltpu.VMEM((z.R, b1, n), f32),
+            pltpu.VMEM((b1, n), f32),
+            pltpu.VMEM((z.C, b1 // z.C, n), f32),
+            pltpu.VMEM((b1 // z.C, n), f32),
             pltpu.SemaphoreType.DMA((n_sem,)),
             pltpu.SemaphoreType.DMA((n_sem,)),
-            pltpu.SemaphoreType.DMA((1,)),
+            pltpu.SemaphoreType.DMA((4,)),
         ],
-        compiler_params=pltpu.CompilerParams(collective_id=1, has_side_effects=True),
-        name="exchange_update",
-    )(part)
+        compiler_params=pltpu.CompilerParams(
+            collective_id=0, has_side_effects=True, vmem_limit_bytes=VMEM_BYTES // 2
+        ),
+        name="gather_factors",
+    )(*ins)
 
 
 def lifted_kernel(z, part, out, got, total, send, recv, keep):
@@ -481,13 +468,17 @@
     return jnp.concatenate([GL[q, idx] for q in range(GL.shape[0])], axis=0)
 
 
-def forward_kernel(z, GL, GR, inv, off, y_ref, part_ref):
+def forward(z, GL, GR, inv, off, y_ref, part_ref):
     b1 = inv.shape[1]
     ys = []
     for k in range(z.R):
         res = GR[k]
         for j in range(k):
-            res = res - mm(group_block(GL, k, j), ys[j])
+            idx = k * (k - 1) // 2 + j
+            low = jnp.concatenate(
+                [GL[core, x, idx] for core in range(CORES) for x in range(z.X)], axis=0
+            )
+            res = res - mm(low, ys[j])
         ys.append(mm(inv[k * b1 : (k + 1) * b1], res))
         y_ref[k * b1 : (k + 1) * b1] = ys[k]
     c = lax.axis_index("col")
@@ -587,10 +578,12 @@
     spb = span // strip
     inv, off = group_diag_inv[0], group_offdiag[0]
     with_root = strip % (8 * z.G * z.C) == 0
-    got = gather_all(z, spb, with_root, group_lower[0], group_rhs[0], group_rows, root_rhs, root_lower)
-    GL, GR, ROWS, RR = got[:4]
-    if with_root:
-        RL = got[4].reshape((z.G * z.C,) + got[4].shape[3:])
+    got = gather_all(
+        z, spb, with_root, group_lower[0], group_rhs[0], group_rows, root_rhs, inv, off, root_lower
+    )
+    GL, ROWS, RR, y, UPD = got[:5]
+    if with_root:
+        RL = got[5].reshape((z.G * z.C,) + got[5].shape[3:])
     else:
         whole = lax.all_gather(root_lower, ("grp", "row", "col"))
         whole = whole.reshape(z.G * z.R, z.C, strip, span)
@@ -598,12 +591,6 @@
             [whole[k * spb + s, j] for k in range(z.C) for s in range(spb) for j in range(k)]
         )[None]
     GL = GL.reshape((z.C,) + GL.shape[2:])
-    y, part = on_chip(
-        functools.partial(forward_kernel, z),
-        [jax.ShapeDtypeStruct((width, n), f32), jax.ShapeDtypeStruct((b1, n), f32)],
-        [], "group_forward", GL, GR, inv, off,
-    )
-    UPD = exchange_update(z, part)
     root_x, lift = on_chip(
         functools.partial(root_kernel, z, spb),
         [jax.ShapeDtypeStruct(root_rhs.shape, f32), jax.ShapeDtypeStruct((n, b1), f32)],

time: 154 us -> 153 us (level)
  Pallas kernels: 153 us -> 138 us
  local copies, waits for them, and re-layouts: 0 us -> 13.7 us
    pallas_call x1 -> x0, Pallas kernels: 23 us -> none  [exchange_update(): pl.pallas_call(functools.partial(update_kernel, z), out_shape=jax.ShapeDt...]
    unnamed x0 -> x26, local copies, waits for them, and re-layouts: none -> 13.7 us
    pallas_call x1, Pallas kernels: 86.4 us -> 99.5 us  [gather_all(): pl.pallas_call(body, out_shape=outs, in_specs=[pl.BlockSpec(memory_space=...]
    pallas_call x3 -> x2, Pallas kernels: 25 us -> 20.4 us  [on_chip(): pl.pallas_call(body, out_shape=out_shape, scratch_shapes=scratch, compile...]
where the time goes in v3:
time: 153 us
  Pallas kernels  138 us (90%)
  local copies, waits for them, and re-layouts  13.7 us (9%)
    pallas_call x1, Pallas kernels, gather_all(): pl.pallas_call(body, out_shape=outs, in_specs=[pl.BlockSpec(memory_space=...  99.5 us
    pallas_call x2, Pallas kernels, on_chip(): pl.pallas_call(body, out_shape=out_shape, scratch_shapes=scratch, compile...  20.4 us
    pallas_call x1, Pallas kernels, exchange_lifted(): pl.pallas_call(functools.partial(lifted_kernel, z), out_shape=jax.ShapeDt...  18.4 us
    unnamed x26, local copies, waits for them, and re-layouts  13.7 us

profile of v3, /device:TPU:0, one launch (start us, length us, event | category | flops | bytes accessed | tf_op | source)
XLA Modules:
  0.0 152.6 jit_solution(14671946409374412235)
XLA Ops:
  0.6 0.0 copy-start.1
  0.6 1.2 copy-done.1
  1.9 0.0 copy-start.5
  1.9 0.9 copy-done.5
  2.8 0.0 copy-start.6
  2.8 1.0 copy-done.6
  3.9 0.0 copy-start.8
  3.9 0.9 copy-done.8
  4.8 0.0 copy-start.9
  4.8 0.9 copy-done.9
  5.7 0.0 copy-start.10
  5.7 0.8 copy-done.10
  6.5 0.0 copy-start.12
  6.5 0.7 copy-done.12
  7.1 99.5 %gather_factors.1 = (f32[2,2,6,64,256]{4,3,2,1,0:T(8,128)S(1)}, s32[2,4,1,256]{3,2,1,0:T(1,128)S(1)}, f32[2,2,2,4,64,128]{5,4,3,2,1,0:T(8,128)S(1)}, f32[1024,12...) custom-call(f32[256,256]{1,0:T(8,128)S(1)} %bitcast.13, ...), custom_call_target="tpu_custom_call" | custom-call | tf_op jit(solution)/shard_map/gather_factors/pallas_call | solution.py:379
  106.6 0.0 copy-start
  106.6 2.6 %copy-done = f32[2,2,2,12,32,512]{5,4,3,2,1,0:T(8,128)} copy-done((f32[2,2,2,12,32,512]{5,4,3,2,1,0:T(8,128)}, f32[2,2,2,12,32,512]{5,4,3,2,1,0:T(8,128)S(1)}, u32[]{:S(2)}) %copy-start) | copy-done | bytes 6291480
  109.2 0.0 copy-start.2
  109.2 1.1 copy-done.2
  110.4 0.0 copy-start.3
  110.4 1.0 copy-done.3
  111.4 0.0 copy-start.4
  111.4 1.0 copy-done.4
  112.4 0.0 copy-start.7
  112.4 0.8 copy-done.7
  113.2 0.0 copy-start.11
  113.2 0.6 copy-done.11
  113.8 15.8 %root_solve.1 = (f32[64,128]{1,0:T(8,128)}, f32[128,256]{1,0:T(8,128)}) custom-call(f32[2,2,2,4,64,128]{5,4,3,2,1,0:T(8,128)} %copy-done.4, s32[2,4,1,256]{3,2,1,0:T(1,128)} %copy-done.11, f32[2,2,2,4,64,128]{5,4,3,2,1,0:T(8,128)} %copy-done.3, f32[8,12,32,512]{3,2,1,0:T(8,128)} %bitcast.7, f32[2048,512]{1,0:T(8,128)} %E.1, s32[1,256]{1,0:T(1,128)} %own_rows.1, ...), custom_call_target="tpu_custom_call" | custom-call | tf_op jit(solution)/shard_map/root_solve/pallas_call | solution.py:563
  129.6 18.4 %exchange_lifted.1.lift = f32[2,2,4,32,256]{4,3,2,1,0:T(8,128)} custom-call(f32[128,256]{1,0:T(8,128)} %get-tuple-element.16.part), custom_call_target="tpu_custom_call" | custom-call | tf_op jit(solution)/shard_map/exchange_lifted/pallas_call | solution.py:449
  148.0 4.5 %group_backward.1 = f32[256,128]{1,0:T(8,128)} custom-call(f32[4,6,64,256]{3,2,1,0:T(8,128)} %bitcast.10, f32[1024,256]{1,0:T(8,128)} %bitcast.8, f32[1024,128]{1,0:T(8,128)} %copy-done.7, f32[2,2,4,32,256]{4,3,2,1,0:T(8,128)} %exchange_lifted.1.lift), custom_call_target="tpu_custom_call" | custom-call | tf_op jit(solution)/shard_map/group_backward/pallas_call | solution.py:563
Async XLA Ops:
  0.6 1.2 copy-start.1
  1.9 0.9 copy-start.5
  2.8 1.0 copy-start.6
  3.9 0.9 copy-start.8
  4.8 0.9 copy-start.9
  5.7 0.8 copy-start.10
  6.5 0.7 copy-start.12
  106.6 2.6 %copy-start = (f32[2,2,2,12,32,512]{5,4,3,2,1,0:T(8,128)}, f32[2,2,2,12,32,512]{5,4,3,2,1,0:T(8,128)S(1)}, u32[]{:S(2)}) copy-start(f32[2,2,2,12,32,512]{5,4,3,2,1,0:T(8,128)S(1)} %get-tuple-element.15) | copy-start | bytes 18874372
  109.2 1.2 copy-start.2
  110.4 1.0 copy-start.3
  111.4 1.0 copy-start.4
  112.4 0.8 copy-start.7
  113.2 0.6 copy-start.11

commit v4 on v3

--- a/solution.py
+++ b/solution.py
@@ -396,7 +396,7 @@
             pltpu.SemaphoreType.DMA((4,)),
         ],
         compiler_params=pltpu.CompilerParams(
-            collective_id=0, has_side_effects=True, vmem_limit_bytes=VMEM_BYTES // 2
+            collective_id=0, has_side_effects=True, vmem_limit_bytes=VMEM_BYTES
         ),
         name="gather_factors",
     )(*ins)

time: 153 us -> 142 us (0.928)
  local copies, waits for them, and re-layouts: 13.7 us -> 0 us
  Pallas kernels: 138 us -> 141 us
    unnamed x26 -> x0, local copies, waits for them, and re-layouts: 13.7 us -> none
    pallas_call x1, Pallas kernels: 99.5 us -> 103 us  [gather_all(): pl.pallas_call(body, out_shape=outs, in_specs=[pl.BlockSpec(memory_space=...]
where the time goes in v4:
time: 142 us
  Pallas kernels  141 us (99%)
    pallas_call x1, Pallas kernels, gather_all(): pl.pallas_call(body, out_shape=outs, in_specs=[pl.BlockSpec(memory_space=...  103 us
    pallas_call x2, Pallas kernels, on_chip(): pl.pallas_call(body, out_shape=out_shape, scratch_shapes=scratch, compile...  20.4 us
    pallas_call x1, Pallas kernels, exchange_lifted(): pl.pallas_call(functools.partial(lifted_kernel, z), out_shape=jax.ShapeDt...  17.9 us

profile of v4, /device:TPU:0, one launch (start us, length us, event | category | flops | bytes accessed | tf_op | source)
XLA Modules:
  0.0 141.6 jit_solution(17613326322455881149)
XLA Ops:
  0.6 102.7 %gather_factors.1 = (f32[2,2,6,64,256]{4,3,2,1,0:T(8,128)}, s32[2,4,1,256]{3,2,1,0:T(1,128)}, f32[2,2,2,4,64,128]{5,4,3,2,1,0:T(8,128)}, f32[1024,128]{1,0:T(8,1...) custom-call(f32[256,256]{1,0:T(8,128)} %bitcast.13, f32[256,128]{1,0:T(8,128)} %bitcast.14, ...), custom_call_target="tpu_custom_call" | custom-call | tf_op jit(solution)/shard_map/gather_factors/pallas_call | solution.py:379
  103.3 15.8 %root_solve.1 = (f32[64,128]{1,0:T(8,128)}, f32[128,256]{1,0:T(8,128)}) custom-call(f32[2,2,2,4,64,128]{5,4,3,2,1,0:T(8,128)} %get-tuple-element.12.UPD, s32[2,4,1,256]{3,2,1,0:T(1,128)} %get-tuple-element.13.ROWS, f32[2,2,2,4,64,128]{5,4,3,2,1,0:T(8,128)} %get-tuple-element.14.RR, f32[8,12,32,512]{3,2,1,0:T(8,128)} %bitcast.7, f32[2048,512]{1,0:T(8,128)} %E.1, ...), custom_call_target="tpu_custom_call" | custom-call | tf_op jit(solution)/shard_map/root_solve/pallas_call | solution.py:563
  119.1 17.9 %exchange_lifted.1.lift = f32[2,2,4,32,256]{4,3,2,1,0:T(8,128)} custom-call(f32[128,256]{1,0:T(8,128)} %get-tuple-element.16.part), custom_call_target="tpu_custom_call" | custom-call | tf_op jit(solution)/shard_map/exchange_lifted/pallas_call | solution.py:449
  137.1 4.5 %group_backward.1 = f32[256,128]{1,0:T(8,128)} custom-call(f32[4,6,64,256]{3,2,1,0:T(8,128)} %bitcast.10, f32[1024,256]{1,0:T(8,128)} %bitcast.9, f32[1024,128]{1,0:T(8,128)} %get-tuple-element.11.y_ref, f32[2,2,4,32,256]{4,3,2,1,0:T(8,128)} %exchange_lifted.1.lift), custom_call_target="tpu_custom_call" | custom-call | tf_op jit(solution)/shard_map/group_backward/pallas_call | solution.py:563
